TPU v7x, 768 devices: a whole 4x8x12 slice. The times are simulated.
768 devices in a mesh: seq: 12 (over z), head: 64 (over x, y, core).
Axes of the slice: x: 4, y: 8, z: 12, core: 2. Of those that a mesh axis runs over, the one named last changes fastest.
Arguments:
- x_in: bfloat16 [6144, 8192], P('seq', 'head'), may hold values from -6 to 6
- gate_in: bfloat16 [6144, 8192], P('seq', 'head'), may hold values from -6 to 6
- b_in: bfloat16 [6144, 128], P('seq'), may hold values from -6 to 6
- c_in: bfloat16 [6144, 128], P('seq'), may hold values from -0.078125 to 0.078125
- log_decay: float32 [128, 6144], P('head', 'seq'), may hold values from -1 to 0
- w_out: bfloat16 [8192, 8192], P(None, 'head'), may hold values from -0.1875 to 0.1875
Outputs:
- mixed: bfloat16 [6144, 8192], P('seq', 'head')
All inputs are finite; a program needn't handle non-finite values.
Results may differ from a plain program's by a relative error of at most 0.0064.
Values may be sent and summed in bfloat16 or wider, within the bound.
A program may use at most 64 MiB of HBM per device.

v0:
```python
import jax
import jax.numpy as jnp
from jax import lax
from jax.sharding import PartitionSpec as P

GROUP = 256


def from_behind(shard, axis, by):
    devices = lax.axis_size(axis)
    pairs = [(i, i + by) for i in range(devices) if 0 <= i + by < devices]
    return lax.ppermute(shard, axis, pairs)


def widen(decays, channels):
    return jnp.repeat(decays, channels, axis=-1)


def per_device(x_in, gate_in, b_in, c_in, log_decay, w_out):
    rows_dev, columns = x_in.shape
    heads_dev = log_decay.shape[0]
    channels = columns // heads_dev
    state_size = b_in.shape[1]
    blocks = rows_dev // GROUP
    inputs_x = x_in.reshape(blocks, GROUP, heads_dev, channels)
    inputs_b = b_in.reshape(blocks, GROUP, state_size)
    inputs_c = c_in.reshape(blocks, GROUP, state_size)
    running = jnp.cumsum(log_decay.reshape(heads_dev, blocks, GROUP), axis=2).transpose(1, 0, 2)
    lower = jnp.tril(jnp.ones((GROUP, GROUP), dtype=bool))
    scores = jnp.einsum("ctn,csn->cts", inputs_c, inputs_b, preferred_element_type=jnp.float32)
    dispersion_amplitude = jnp.where(lower, running[:, :, :, None] - running[:, :, None, :], 0.0)
    weights = jnp.where(lower, scores[:, None] * jnp.exp(dispersion_amplitude), 0.0).astype(
        jnp.bfloat16
    )
    y_diag = jnp.einsum("chts,cshp->cthp", weights, inputs_x, preferred_element_type=jnp.float32)
    last_cum = running[:, :, -1:]
    b_scaled = (
        inputs_b.astype(jnp.float32)[:, None] * jnp.exp(last_cum - running)[..., None]
    ).astype(jnp.bfloat16)
    local_state = jnp.einsum(
        "chtn,cthp->cnhp", b_scaled, inputs_x, preferred_element_type=jnp.float32
    )
    local_state = local_state.reshape(blocks, state_size, columns)
    totals = jnp.exp(last_cum[..., 0])
    starts = []
    reaches = []
    carried = jnp.zeros((state_size, columns), jnp.float32)
    reach = jnp.ones((heads_dev,), jnp.float32)
    for index in range(blocks):
        starts.append(carried)
        reaches.append(reach)
        carried = carried * widen(totals[index], channels)[None] + local_state[index]
        reach = reach * totals[index]

    def advance(position, incoming):
        outgoing = carried + incoming * widen(reach, channels)[None]
        return from_behind(outgoing, "seq", 1)

    incoming = lax.fori_loop(
        0, lax.axis_size("seq") - 1, advance, jnp.zeros((state_size, columns), jnp.float32)
    )
    start_full = (
        jnp.stack(starts) + incoming[None] * widen(jnp.stack(reaches), channels)[:, None, :]
    )
    start_bf = start_full.astype(jnp.bfloat16)
    y_carry = jnp.einsum("ctn,cnk->ctk", inputs_c, start_bf, preferred_element_type=jnp.float32)
    y_carry = y_carry * widen(jnp.exp(running).transpose(0, 2, 1), channels)
    mixed = y_diag.reshape(blocks, GROUP, columns) + y_carry
    gated = (mixed.reshape(rows_dev, columns) * jax.nn.silu(gate_in.astype(jnp.float32))).astype(
        jnp.bfloat16
    )
    own_rows = lax.all_to_all(w_out, "head", split_axis=0, concat_axis=1, tiled=True)
    partial_value = jnp.dot(gated, own_rows, preferred_element_type=jnp.float32)
    result = lax.psum_scatter(partial_value, "head", scatter_dimension=1, tiled=True)
    return result.astype(jnp.bfloat16)


def solution(mesh):
    in_specs = (
        P("seq", "head"),
        P("seq", "head"),
        P("seq", None),
        P("seq", None),
        P("head", "seq"),
        P(None, "head"),
    )
    out_specs = P("seq", "head")
    return jax.shard_map(
        per_device, mesh=mesh, in_specs=in_specs, out_specs=out_specs, check_vma=False
    )
```

profile of v0, /device:TPU:1, one launch (start us, length us, event | category | flops | bytes accessed | tf_op | source)
XLA Modules:
  0.0 335.0 jit_solution(8860951374147190199)
XLA Ops:
  6.5 14.8 %all-to-all-start = ((bf16[64,128,128]{2,1,0:T(8,128)(2,1)}), bf16[64,128,128]{2,1,0:T(8,128)(2,1)S(1)}, u32[]{:S(2)}, u32[]{:S(2)}) async-start(bf16[64,128,128]{2,1,0:T(8,128)(2,1)} %bitcast.50), calls=%async_computation | async-start | bytes 4194304 | tf_op jit(solution)/shard_map/all_to_all | solution.py:72
  21.4 1.2 reduce-window.6
  23.8 0.3 convolution_bitcast_fusion.1
  24.9 67.3 %while.10 = (s32[]{:T(128)}, f32[128,128]{1,0:T(8,128)S(1)}, f32[2]{0:T(128)S(1)}, f32[128,128]{1,0:T(8,128)S(1)}, s32[]{:T(128)}) while((s32[]{:T(128)}, f32[128,128]{1,0:T(8,128)S(1)}, f32[2]{0:T(128)S(1)}, f32[128,128]{1,0:T(8,128)S(1)}, s32[]{:T(128)}) %tuple.22), condition=%wide.region_3.4_spmd, body=%wide.region_2.3_spmd.sunk | while | flops 32770 | bytes 460909 | solution.py:59
  25.1 1.3 collective-permute-start
  26.4 1.3 collective-permute-done
  27.9 4.0 %collective-permute-start = (f32[128,128]{1,0:T(8,128)S(1)}, f32[128,128]{1,0:T(8,128)S(1)}, u32[]{:S(2)}, u32[]{:S(2)}) collective-permute-start(f32[128,128]{1,0:T(8,128)S(1)} %multiply_add_fusion.3), channel_id=1, source_target_pairs={{0,64},{64,128},{128,192},{192,256},{256,320},{320,384},{384,448},... | collective-permute-start | bytes 196616 | tf_op jit(solution)/shard_map/while/body/eval_jaxpr/ppermute | solution.py:12
  31.9 1.3 collective-permute-done
  33.4 4.0 %collective-permute-start = (f32[128,128]{1,0:T(8,128)S(1)}, f32[128,128]{1,0:T(8,128)S(1)}, u32[]{:S(2)}, u32[]{:S(2)}) collective-permute-start(f32[128,128]{1,0:T(8,128)S(1)} %multiply_add_fusion.3), channel_id=1, source_target_pairs={{0,64},{64,128},{128,192},{192,256},{256,320},{320,384},{384,448},... | collective-permute-start | bytes 196616 | tf_op jit(solution)/shard_map/while/body/eval_jaxpr/ppermute | solution.py:12
  37.4 1.3 collective-permute-done
  38.8 4.9 %collective-permute-start = (f32[128,128]{1,0:T(8,128)S(1)}, f32[128,128]{1,0:T(8,128)S(1)}, u32[]{:S(2)}, u32[]{:S(2)}) collective-permute-start(f32[128,128]{1,0:T(8,128)S(1)} %multiply_add_fusion.3), channel_id=1, source_target_pairs={{0,64},{64,128},{128,192},{192,256},{256,320},{320,384},{384,448},... | collective-permute-start | bytes 196616 | tf_op jit(solution)/shard_map/while/body/eval_jaxpr/ppermute | solution.py:12
  43.8 1.3 collective-permute-done
  45.2 5.2 %collective-permute-start = (f32[128,128]{1,0:T(8,128)S(1)}, f32[128,128]{1,0:T(8,128)S(1)}, u32[]{:S(2)}, u32[]{:S(2)}) collective-permute-start(f32[128,128]{1,0:T(8,128)S(1)} %multiply_add_fusion.3), channel_id=1, source_target_pairs={{0,64},{64,128},{128,192},{192,256},{256,320},{320,384},{384,448},... | collective-permute-start | bytes 196616 | tf_op jit(solution)/shard_map/while/body/eval_jaxpr/ppermute | solution.py:12
  50.4 1.3 collective-permute-done
  51.9 5.2 %collective-permute-start = (f32[128,128]{1,0:T(8,128)S(1)}, f32[128,128]{1,0:T(8,128)S(1)}, u32[]{:S(2)}, u32[]{:S(2)}) collective-permute-start(f32[128,128]{1,0:T(8,128)S(1)} %multiply_add_fusion.3), channel_id=1, source_target_pairs={{0,64},{64,128},{128,192},{192,256},{256,320},{320,384},{384,448},... | collective-permute-start | bytes 196616 | tf_op jit(solution)/shard_map/while/body/eval_jaxpr/ppermute | solution.py:12
  57.1 1.3 collective-permute-done
  58.6 5.2 %collective-permute-start = (f32[128,128]{1,0:T(8,128)S(1)}, f32[128,128]{1,0:T(8,128)S(1)}, u32[]{:S(2)}, u32[]{:S(2)}) collective-permute-start(f32[128,128]{1,0:T(8,128)S(1)} %multiply_add_fusion.3), channel_id=1, source_target_pairs={{0,64},{64,128},{128,192},{192,256},{256,320},{320,384},{384,448},... | collective-permute-start | bytes 196616 | tf_op jit(solution)/shard_map/while/body/eval_jaxpr/ppermute | solution.py:12
  63.8 1.3 collective-permute-done
  65.3 5.2 %collective-permute-start = (f32[128,128]{1,0:T(8,128)S(1)}, f32[128,128]{1,0:T(8,128)S(1)}, u32[]{:S(2)}, u32[]{:S(2)}) collective-permute-start(f32[128,128]{1,0:T(8,128)S(1)} %multiply_add_fusion.3), channel_id=1, source_target_pairs={{0,64},{64,128},{128,192},{192,256},{256,320},{320,384},{384,448},... | collective-permute-start | bytes 196616 | tf_op jit(solution)/shard_map/while/body/eval_jaxpr/ppermute | solution.py:12
  70.5 1.3 collective-permute-done
  72.0 5.2 %collective-permute-start = (f32[128,128]{1,0:T(8,128)S(1)}, f32[128,128]{1,0:T(8,128)S(1)}, u32[]{:S(2)}, u32[]{:S(2)}) collective-permute-start(f32[128,128]{1,0:T(8,128)S(1)} %multiply_add_fusion.3), channel_id=1, source_target_pairs={{0,64},{64,128},{128,192},{192,256},{256,320},{320,384},{384,448},... | collective-permute-start | bytes 196616 | tf_op jit(solution)/shard_map/while/body/eval_jaxpr/ppermute | solution.py:12
  77.2 1.7 collective-permute-done
  79.0 5.2 %collective-permute-start = (f32[128,128]{1,0:T(8,128)S(1)}, f32[128,128]{1,0:T(8,128)S(1)}, u32[]{:S(2)}, u32[]{:S(2)}) collective-permute-start(f32[128,128]{1,0:T(8,128)S(1)} %multiply_add_fusion.3), channel_id=1, source_target_pairs={{0,64},{64,128},{128,192},{192,256},{256,320},{320,384},{384,448},... | collective-permute-start | bytes 196616 | tf_op jit(solution)/shard_map/while/body/eval_jaxpr/ppermute | solution.py:12
  84.2 1.3 collective-permute-done
  85.7 5.2 %collective-permute-start = (f32[128,128]{1,0:T(8,128)S(1)}, f32[128,128]{1,0:T(8,128)S(1)}, u32[]{:S(2)}, u32[]{:S(2)}) collective-permute-start(f32[128,128]{1,0:T(8,128)S(1)} %multiply_add_fusion.3), channel_id=1, source_target_pairs={{0,64},{64,128},{128,192},{192,256},{256,320},{320,384},{384,448},... | collective-permute-start | bytes 196616 | tf_op jit(solution)/shard_map/while/body/eval_jaxpr/ppermute | solution.py:12
  90.9 1.3 collective-permute-done
  92.7 0.5 fusion.2
  93.7 1.3 copy-done.1
  95.0 3.2 copy.59
  98.2 8.1 %fusion.21 = f32[512,8192]{1,0:T(8,128)} fusion(bf16[512,128]{1,0:T(8,128)(2,1)S(1)} %fusion.14, bf16[128,8192]{0,1:T(8,128)(2,1)S(1)} %bitcast.48), kind=kOutput, calls=%fused_computation.41 | convolution fusion | flops 1073741824 | bytes 19005440 | tf_op jit(solution)/shard_map/dot_general | solution.py:73
  106.3 220.2 %reduce-scatter.2.cloned.1.call-done = f32[512,128]{1,0:T(8,128)} async-done(((f32[512,8192]{1,0:T(8,128)}), f32[512,128]{1,0:T(8,128)}) %reduce-scatter.2.cloned.1.call-update) | async-done | bytes 262160 | tf_op jit(solution)/shard_map/reduce_scatter | solution.py:74
  326.5 1.6 convert_element_type.31
  (81 shorter events, 4.7 us)
Async XLA Ops:
  6.5 85.9 %copy-start = (bf16[512,128]{1,0:T(8,128)(2,1)S(1)}, bf16[512,128]{1,0:T(8,128)(2,1)}, u32[]{:S(2)}) copy-start(bf16[512,128]{1,0:T(8,128)(2,1)} %param.11) | copy-start | bytes 393220
  6.5 14.8 %copy-start.5 = (f32[2,512]{1,0:T(2,128)S(1)}, f32[2,512]{1,0:T(2,128)}, u32[]{:S(2)}) copy-start(f32[2,512]{1,0:T(2,128)} %param.12) | copy-start | bytes 12292
  6.5 17.0 %copy-start.3 = (bf16[512,128]{1,0:T(8,128)(2,1)S(1)}, bf16[512,128]{1,0:T(8,128)(2,1)}, u32[]{:S(2)}) copy-start(bf16[512,128]{1,0:T(8,128)(2,1)} %param.8) | copy-start | bytes 393220
  6.5 17.3 %copy-start.2 = (bf16[512,128]{1,0:T(8,128)(2,1)S(1)}, bf16[512,128]{1,0:T(8,128)(2,1)}, u32[]{:S(2)}) copy-start(bf16[512,128]{1,0:T(8,128)(2,1)} %param.10) | copy-start | bytes 393220
  6.5 87.1 %all-to-all-start = ((bf16[64,128,128]{2,1,0:T(8,128)(2,1)}), bf16[64,128,128]{2,1,0:T(8,128)(2,1)S(1)}, u32[]{:S(2)}, u32[]{:S(2)}) async-start(bf16[64,128,128]{2,1,0:T(8,128)(2,1)} %bitcast.50), calls=%async_computation | async-start | bytes 4194304 | tf_op jit(solution)/shard_map/all_to_all | solution.py:72
  21.3 305.2 %reduce-scatter.2.cloned.1.call-start = ((), (), s32[]{:S(2)}) async-start(), calls=%async_computation.2 | async-start | bytes 17039360 | tf_op jit(solution)/shard_map/reduce_scatter | solution.py:74
  25.1 2.6 collective-permute-start
  27.9 5.3 %collective-permute-start = (f32[128,128]{1,0:T(8,128)S(1)}, f32[128,128]{1,0:T(8,128)S(1)}, u32[]{:S(2)}, u32[]{:S(2)}) collective-permute-start(f32[128,128]{1,0:T(8,128)S(1)} %multiply_add_fusion.3), channel_id=1, source_target_pairs={{0,64},{64,128},{128,192},{192,256},{256,320},{320,384},{384,448},... | collective-permute-start | bytes 196616 | tf_op jit(solution)/shard_map/while/body/eval_jaxpr/ppermute | solution.py:12
  33.4 5.3 %collective-permute-start = (f32[128,128]{1,0:T(8,128)S(1)}, f32[128,128]{1,0:T(8,128)S(1)}, u32[]{:S(2)}, u32[]{:S(2)}) collective-permute-start(f32[128,128]{1,0:T(8,128)S(1)} %multiply_add_fusion.3), channel_id=1, source_target_pairs={{0,64},{64,128},{128,192},{192,256},{256,320},{320,384},{384,448},... | collective-permute-start | bytes 196616 | tf_op jit(solution)/shard_map/while/body/eval_jaxpr/ppermute | solution.py:12
  38.8 6.2 %collective-permute-start = (f32[128,128]{1,0:T(8,128)S(1)}, f32[128,128]{1,0:T(8,128)S(1)}, u32[]{:S(2)}, u32[]{:S(2)}) collective-permute-start(f32[128,128]{1,0:T(8,128)S(1)} %multiply_add_fusion.3), channel_id=1, source_target_pairs={{0,64},{64,128},{128,192},{192,256},{256,320},{320,384},{384,448},... | collective-permute-start | bytes 196616 | tf_op jit(solution)/shard_map/while/body/eval_jaxpr/ppermute | solution.py:12
  45.2 6.5 %collective-permute-start = (f32[128,128]{1,0:T(8,128)S(1)}, f32[128,128]{1,0:T(8,128)S(1)}, u32[]{:S(2)}, u32[]{:S(2)}) collective-permute-start(f32[128,128]{1,0:T(8,128)S(1)} %multiply_add_fusion.3), channel_id=1, source_target_pairs={{0,64},{64,128},{128,192},{192,256},{256,320},{320,384},{384,448},... | collective-permute-start | bytes 196616 | tf_op jit(solution)/shard_map/while/body/eval_jaxpr/ppermute | solution.py:12
  51.9 6.5 %collective-permute-start = (f32[128,128]{1,0:T(8,128)S(1)}, f32[128,128]{1,0:T(8,128)S(1)}, u32[]{:S(2)}, u32[]{:S(2)}) collective-permute-start(f32[128,128]{1,0:T(8,128)S(1)} %multiply_add_fusion.3), channel_id=1, source_target_pairs={{0,64},{64,128},{128,192},{192,256},{256,320},{320,384},{384,448},... | collective-permute-start | bytes 196616 | tf_op jit(solution)/shard_map/while/body/eval_jaxpr/ppermute | solution.py:12
  58.6 6.5 %collective-permute-start = (f32[128,128]{1,0:T(8,128)S(1)}, f32[128,128]{1,0:T(8,128)S(1)}, u32[]{:S(2)}, u32[]{:S(2)}) collective-permute-start(f32[128,128]{1,0:T(8,128)S(1)} %multiply_add_fusion.3), channel_id=1, source_target_pairs={{0,64},{64,128},{128,192},{192,256},{256,320},{320,384},{384,448},... | collective-permute-start | bytes 196616 | tf_op jit(solution)/shard_map/while/body/eval_jaxpr/ppermute | solution.py:12
  65.3 6.5 %collective-permute-start = (f32[128,128]{1,0:T(8,128)S(1)}, f32[128,128]{1,0:T(8,128)S(1)}, u32[]{:S(2)}, u32[]{:S(2)}) collective-permute-start(f32[128,128]{1,0:T(8,128)S(1)} %multiply_add_fusion.3), channel_id=1, source_target_pairs={{0,64},{64,128},{128,192},{192,256},{256,320},{320,384},{384,448},... | collective-permute-start | bytes 196616 | tf_op jit(solution)/shard_map/while/body/eval_jaxpr/ppermute | solution.py:12
  72.0 6.9 %collective-permute-start = (f32[128,128]{1,0:T(8,128)S(1)}, f32[128,128]{1,0:T(8,128)S(1)}, u32[]{:S(2)}, u32[]{:S(2)}) collective-permute-start(f32[128,128]{1,0:T(8,128)S(1)} %multiply_add_fusion.3), channel_id=1, source_target_pairs={{0,64},{64,128},{128,192},{192,256},{256,320},{320,384},{384,448},... | collective-permute-start | bytes 196616 | tf_op jit(solution)/shard_map/while/body/eval_jaxpr/ppermute | solution.py:12
  79.0 6.5 %collective-permute-start = (f32[128,128]{1,0:T(8,128)S(1)}, f32[128,128]{1,0:T(8,128)S(1)}, u32[]{:S(2)}, u32[]{:S(2)}) collective-permute-start(f32[128,128]{1,0:T(8,128)S(1)} %multiply_add_fusion.3), channel_id=1, source_target_pairs={{0,64},{64,128},{128,192},{192,256},{256,320},{320,384},{384,448},... | collective-permute-start | bytes 196616 | tf_op jit(solution)/shard_map/while/body/eval_jaxpr/ppermute | solution.py:12
  85.7 6.5 %collective-permute-start = (f32[128,128]{1,0:T(8,128)S(1)}, f32[128,128]{1,0:T(8,128)S(1)}, u32[]{:S(2)}, u32[]{:S(2)}) collective-permute-start(f32[128,128]{1,0:T(8,128)S(1)} %multiply_add_fusion.3), channel_id=1, source_target_pairs={{0,64},{64,128},{128,192},{192,256},{256,320},{320,384},{384,448},... | collective-permute-start | bytes 196616 | tf_op jit(solution)/shard_map/while/body/eval_jaxpr/ppermute | solution.py:12
  92.7 0.9 copy-start.4
  93.7 1.3 copy-start.1
Sparse Core Ops, SparseCore 0:
  106.5 219.9 reduce-scatter.1
where the time goes:
time: 338 us; the launch traced here: 335 us
  waiting for transfers between devices  235 us (70%)
  starting transfers between devices  65.4 us (19%)
  between operations  13.6 us (4%)
  matrix products  9.34 us (3%)
  local copies, waits for them, and re-layouts  7.82 us (2%)
  other arithmetic  3.72 us (1%)
    reduce_scatter x1, waiting for transfers between devices, per_device(): lax.psum_scatter(partial_value, 'head', scatter_dimension=1, tiled=True)  220 us
    ppermute x11, starting transfers between devices, from_behind(): return lax.ppermute(shard, axis, pairs)  50.5 us
    all_to_all x1, starting transfers between devices, per_device(): lax.all_to_all(w_out, 'head', split_axis=0, concat_axis=1, tiled=True)  14.8 us
    ppermute x11, waiting for transfers between devices, from_behind(): return lax.ppermute(shard, axis, pairs)  14.7 us
    dot_general x1, matrix products, per_device(): partial_value = jnp.dot(gated, own_rows, preferred_element_type=jnp.float32)  8.08 us
  transfers between devices with their start and end apart: 13, of which 12 were waited for; matrix products, arithmetic and copies ran while one was open for 2% of the time, Pallas kernels for 0%

commit v1 on v0

v1 whole, which is shorter than its diff:
```python
import functools

import jax
import jax.numpy as jnp
from jax import lax
from jax.experimental import pallas as pl
from jax.experimental.pallas import tpu as pltpu
from jax.sharding import PartitionSpec as P

MESH = pl.DeviceIdType.MESH
BLOCK = 256
NX, NY, NC = 4, 8, 2
SPAN = 4
CHUNKS = 4
NT = (((1,), (1,)), ((), ()))
TN = (((0,), (0,)), ((), ()))
F32 = jnp.float32
BF16 = jnp.bfloat16


def exact(a, b):
    return lax.dot_general(a, b, NT, precision=lax.Precision.HIGHEST, preferred_element_type=F32)


def pack(ref, state, total):
    n = state.shape[0]
    row = lax.broadcasted_iota(jnp.int32, (16, state.shape[1]), 0)
    high = total.astype(BF16).astype(F32)
    tail = jnp.where(row == 0, high, jnp.where(row == 1, total - high, 0.0))
    ref[0:n, :] = state.astype(BF16)
    ref[n : n + 16, :] = tail.astype(BF16)


def unpack(ref, n):
    tail = ref[n : n + 16, :].astype(F32)
    return ref[0:n, :].astype(F32), tail[0:1] + tail[1:2]


def kernel(
    seq_size,
    x_ref,
    gate_ref,
    b_ref,
    c_ref,
    decay_ref,
    w_ref,
    out_ref,
    m1,
    m2,
    m2_in,
    diag,
    wide,
    blocks,
    w_buf,
    total,
    part,
    part_in,
    m1_s,
    m1_r,
    m2_s,
    m2_r,
    w_s,
    w_r,
    own_s,
    ring_s,
    ring_r,
    twin_s,
    twin_r,
    part_s,
    part_r,
):
    rows, columns = x_ref.shape
    states = b_ref.shape[1]
    channels = columns // decay_ref.shape[0]
    step = rows // CHUNKS
    s = lax.axis_index("seq")
    head = lax.axis_index("head")
    px, py, core = head // (NY * NC), (head // NC) % NY, head % NC
    group, place = s // SPAN, s % SPAN

    def device(z, x, y, c):
        return (z, (x * NY + y) * NC + c)

    mates = [(place + i) % SPAN for i in range(1, SPAN)]
    mate_ids = [device(group * SPAN + m, px, py, core) for m in mates]
    ahead_ids = [device((s + SPAN * i) % seq_size, px, py, core) for i in (1, 2)]
    peers = [(px + i) % NX for i in range(1, NX)]
    peer_ids = [device(s, p, py, core) for p in peers]
    up = device(s, px, (py + 1) % NY, core)
    down = device(s, px, (py + NY - 1) % NY, core)
    twin = device(s, px, py, 1 - core)

    def remote(src, dst, send, recv, to):
        return pltpu.make_async_remote_copy(
            src_ref=src, dst_ref=dst, send_sem=send, recv_sem=recv, device_id=to, device_id_type=MESH
        )

    partners = mate_ids + ahead_ids + peer_ids + [up, down, twin]
    barrier = pltpu.get_barrier_semaphore()
    for to in partners:
        pl.semaphore_signal(barrier, inc=1, device_id=to, device_id_type=MESH)

    depth = NY * NC * columns
    own_w = pltpu.make_async_copy(w_ref.at[pl.ds(px * depth, depth), :], w_buf.at[px], own_s)
    own_w.start()
    t_of = lax.broadcasted_iota(jnp.int32, (BLOCK, BLOCK), 0)
    s_of = lax.broadcasted_iota(jnp.int32, (BLOCK, BLOCK), 1)
    lower = s_of <= t_of
    ones = jnp.where(lower, 1.0, 0.0)
    first_head = lax.broadcasted_iota(jnp.int32, (BLOCK, columns), 1) < channels
    first_row = lax.broadcasted_iota(jnp.int32, (columns, BLOCK), 0) < channels
    local, cum_last = [], []
    for q in range(rows // BLOCK):
        at = slice(q * BLOCK, (q + 1) * BLOCK)
        decay = decay_ref[:, at]
        cum = exact(ones, jnp.where(first_row, decay[0:1], decay[1:2]))
        wide[at, :] = cum
        last = cum[BLOCK - 1 :, :]
        to_end = jnp.exp(last - cum)
        b = b_ref[at, :].astype(F32)
        x = x_ref[at, :]
        halves = [
            lax.dot_general(
                (b * to_end[:, h * channels : h * channels + 1]).astype(BF16),
                x,
                TN,
                preferred_element_type=F32,
            )
            for h in range(2)
        ]
        local.append(jnp.where(first_head[:states], halves[0], halves[1]))
        cum_last.append(last)
    m1_own = m1.at[place]
    pack(
        m1_own,
        local[0] * jnp.exp(cum_last[1]) + local[1],
        jnp.exp(cum_last[0] + cum_last[1]),
    )

    pl.semaphore_wait(barrier, len(partners))
    sent = []
    for i, to in enumerate(mate_ids):
        copy = remote(m1_own, m1_own, m1_s.at[i], m1_r.at[i], to)
        copy.start()
        sent.append(copy)
    for i, to in enumerate(peer_ids):
        copy = remote(
            w_ref.at[pl.ds(peers[i] * depth, depth), :], w_buf.at[px], w_s.at[i], w_r.at[i], to
        )
        copy.start()
        sent.append(copy)

    for q in range(rows // BLOCK):
        at = slice(q * BLOCK, (q + 1) * BLOCK)
        decay = decay_ref[:, at]
        cum = wide[at, :]
        x = x_ref[at, :]
        scores = lax.dot_general(c_ref[at, :], b_ref[at, :], NT, preferred_element_type=F32)
        along = exact(jnp.where(first_row[56:72], decay[0:1], decay[1:2]), ones)
        halves = []
        for h in range(2):
            gap = cum[:, h * channels : h * channels + 1] - along[8 * h : 8 * h + 1, :]
            weights = jnp.where(lower, scores * jnp.exp(jnp.where(lower, gap, 0.0)), 0.0)
            halves.append(jnp.dot(weights.astype(BF16), x, preferred_element_type=F32))
        diag[at, :] = jnp.where(first_head, halves[0], halves[1])

    for i in range(SPAN - 1):
        slot = m1.at[(place + SPAN - 1 - i) % SPAN]
        remote(slot, slot, m1_s.at[i], m1_r.at[i], mate_ids[i]).wait_recv()
    state = jnp.zeros((states, columns), F32)
    decayed = jnp.ones((1, columns), F32)
    before, before_decay = state, decayed
    for i in range(SPAN):
        before = jnp.where(place == i, state, before)
        before_decay = jnp.where(place == i, decayed, before_decay)
        more, its_decay = unpack(m1.at[i], states)
        state = state * its_decay + more
        decayed = decayed * its_decay
    pack(m2, state, decayed)
    for i, to in enumerate(ahead_ids):
        copy = remote(m2, m2_in.at[i], m2_s.at[i], m2_r.at[i], to)
        copy.start()
        sent.append(copy)
    for i, to in enumerate(ahead_ids):
        remote(m2, m2_in.at[i], m2_s.at[i], m2_r.at[i], to).wait_recv()
    near, near_decay = unpack(m2_in.at[0], states)
    far, _ = unpack(m2_in.at[1], states)
    earlier = jnp.where(group >= 2, far * near_decay, 0.0) + near
    start = before + jnp.where(group >= 1, earlier * before_decay, 0.0)
    starts = [start, start * jnp.exp(cum_last[0]) + local[0]]

    mine = py * NC + core
    for r in range(CHUNKS):
        at = slice(r * step, (r + 1) * step)
        start_bf = starts[r * step // BLOCK].astype(BF16)
        carry = jnp.dot(c_ref[at, :], start_bf, preferred_element_type=F32)
        y = diag[at, :] + carry * jnp.exp(wide[at, :])
        gate = gate_ref[at, :].astype(F32)
        blocks[mine, at, :] = (y * (gate / (1.0 + jnp.exp(-gate)))).astype(BF16)
        here = blocks.at[mine, at]
        for d, to in enumerate((up, down)):
            copy = remote(here, here, ring_s.at[r, d, 0], ring_r.at[r, d, 0], to)
            copy.start()
            sent.append(copy)
        copy = remote(here, here, twin_s.at[r, 0], twin_r.at[r, 0], twin)
        copy.start()
        sent.append(copy)

    def hops(r, d):
        return NY // 2 if (r + d) % 2 == 0 else NY // 2 - 1

    def behind(hop, d):
        return (py + NY - hop) % NY if d == 0 else (py + hop) % NY

    for hop in range(1, NY // 2 + 1):
        for r in range(CHUNKS):
            at = slice(r * step, (r + 1) * step)
            for d, to in enumerate((up, down)):
                if hop > hops(r, d):
                    continue
                here = blocks.at[behind(hop, d) * NC + core, at]
                remote(here, here, ring_s.at[r, d, hop - 1], ring_r.at[r, d, hop - 1], to).wait_recv()
                if hop < hops(r, d):
                    copy = remote(here, here, ring_s.at[r, d, hop], ring_r.at[r, d, hop], to)
                    copy.start()
                    sent.append(copy)
                which = 2 * hop - 1 + d if hop < NY // 2 else NY - 1
                copy = remote(here, here, twin_s.at[r, which], twin_r.at[r, which], twin)
                copy.start()
                sent.append(copy)

    own_w.wait()
    for i in range(NX - 1):
        slot = w_buf.at[(px + NX - 1 - i) % NX]
        remote(slot, slot, w_s.at[i], w_r.at[i], peer_ids[i]).wait_recv()
    for r in range(CHUNKS):
        at = slice(r * step, (r + 1) * step)
        for which in range(NY):
            if which == 0:
                where = py
            elif which < NY - 1:
                where = behind((which + 1) // 2, (which + 1) % 2)
            else:
                where = (py + NY // 2) % NY
            there = blocks.at[where * NC + 1 - core, at]
            remote(there, there, twin_s.at[r, which], twin_r.at[r, which], twin).wait_recv()
        gathered = jnp.concatenate([blocks[k, at, :] for k in range(NY * NC)], axis=1)
        for i, to in enumerate(peer_ids):
            part[i, at, :] = jnp.dot(
                gathered, w_buf[peers[i]], preferred_element_type=F32
            ).astype(BF16)
            copy = remote(part.at[i, at], part_in.at[i, at], part_s.at[i, r], part_r.at[i, r], to)
            copy.start()
            sent.append(copy)
        total[at, :] = jnp.dot(gathered, w_buf[px], preferred_element_type=F32)
    for r in range(CHUNKS):
        at = slice(r * step, (r + 1) * step)
        for i, to in enumerate(peer_ids):
            remote(part.at[i, at], part_in.at[i, at], part_s.at[i, r], part_r.at[i, r], to).wait_recv()
        value = total[at, :]
        for i in range(NX - 1):
            value = value + part_in[i, at, :].astype(F32)
        out_ref[at, :] = value.astype(BF16)
    for copy in sent:
        copy.wait_send()


def per_device(seq_size, x_in, gate_in, b_in, c_in, log_decay, w_out):
    rows, columns = x_in.shape
    states = b_in.shape[1]
    depth = NY * NC * columns
    dma = pltpu.SemaphoreType.DMA
    vmem = pl.BlockSpec(memory_space=pltpu.VMEM)
    return pl.pallas_call(
        functools.partial(kernel, seq_size),
        out_shape=jax.ShapeDtypeStruct((rows, columns), BF16),
        in_specs=[vmem] * 5 + [pl.BlockSpec(memory_space=pl.ANY)],
        out_specs=vmem,
        scratch_shapes=[
            pltpu.VMEM((SPAN, states + 16, columns), BF16),
            pltpu.VMEM((states + 16, columns), BF16),
            pltpu.VMEM((2, states + 16, columns), BF16),
            pltpu.VMEM((rows, columns), F32),
            pltpu.VMEM((rows, columns), F32),
            pltpu.VMEM((NY * NC, rows, columns), BF16),
            pltpu.VMEM((NX, depth, columns), BF16),
            pltpu.VMEM((rows, columns), F32),
            pltpu.VMEM((NX - 1, rows, columns), BF16),
            pltpu.VMEM((NX - 1, rows, columns), BF16),
            dma((SPAN - 1,)),
            dma((SPAN - 1,)),
            dma((2,)),
            dma((2,)),
            dma((NX - 1,)),
            dma((NX - 1,)),
            dma(()),
            dma((CHUNKS, 2, NY // 2)),
            dma((CHUNKS, 2, NY // 2)),
            dma((CHUNKS, NY)),
            dma((CHUNKS, NY)),
            dma((NX - 1, CHUNKS)),
            dma((NX - 1, CHUNKS)),
        ],
        compiler_params=pltpu.CompilerParams(
            collective_id=0, has_side_effects=True, vmem_limit_bytes=40 * 2**20
        ),
        name="ssd_layer",
    )(x_in, gate_in, b_in, c_in, log_decay, w_out)


def solution(mesh):
    in_specs = (
        P("seq", "head"),
        P("seq", "head"),
        P("seq", None),
        P("seq", None),
        P("head", "seq"),
        P(None, "head"),
    )
    return jax.shard_map(
        functools.partial(per_device, mesh.shape["seq"]),
        mesh=mesh,
        in_specs=in_specs,
        out_specs=P("seq", "head"),
        check_vma=False,
    )
```

time: 338 us -> 60 us (0.18)
  waiting for transfers between devices: 235 us -> 0 us
  starting transfers between devices: 65.4 us -> 0 us
  Pallas kernels: 0 us -> 53.2 us
  between operations: 13.6 us -> 0.02 us
  matrix products: 9.34 us -> 0 us
  other arithmetic: 3.72 us -> 0 us
    reduce_scatter x1 -> x0, waiting for transfers between devices: 220 us -> none  [per_device(): lax.psum_scatter(partial_value, 'head', scatter_dimension=1, tiled=True)]
    pallas_call x0 -> x1, Pallas kernels: none -> 53.2 us  [per_device(): pl.pallas_call(functools.partial(kernel, seq_size), out_shape=jax.ShapeDt...]
    ppermute x11 -> x0, starting transfers between devices: 50.5 us -> none  [from_behind(): return lax.ppermute(shard, axis, pairs)]
    all_to_all x1 -> x0, starting transfers between devices: 14.8 us -> none  [per_device(): lax.all_to_all(w_out, 'head', split_axis=0, concat_axis=1, tiled=True)]
    ppermute x11 -> x0, waiting for transfers between devices: 14.7 us -> none  [from_behind(): return lax.ppermute(shard, axis, pairs)]
    dot_general x5 -> x0, matrix products: 9.34 us -> none  [the longest x1 8.08 us: per_device(): partial_value = jnp.dot(gated, own_rows, preferred_element_type=jnp.float32)]
    unnamed x12 -> x13, local copies, waits for them, and re-layouts: 1.39 us -> 6.55 us
  transfers between devices with their start and end apart: 13 -> 0, of which waited for: 12 -> 0; matrix products, arithmetic and copies ran while one was open for 2% -> 0% of each run, Pallas kernels for 0% -> 0%
where the time goes in v1:
time: 60 us; the launch traced here: 59.7 us
  Pallas kernels  53.2 us (89%)
  local copies, waits for them, and re-layouts  6.55 us (11%)
    pallas_call x1, Pallas kernels, per_device(): pl.pallas_call(functools.partial(kernel, seq_size), out_shape=jax.ShapeDt...  53.2 us
    unnamed x13, local copies, waits for them, and re-layouts  6.55 us

profile of v1, /device:TPU:1, one launch (start us, length us, event | category | flops | bytes accessed | tf_op | source)
XLA Modules:
  0.0 59.7 jit_solution(4617421146635556281)
XLA Ops:
  0.0 0.0 copy-start
  0.0 1.6 %copy-done = bf16[8192,128]{1,0:T(8,128)(2,1)S(1)} copy-done((bf16[8192,128]{1,0:T(8,128)(2,1)S(1)}, bf16[8192,128]{1,0:T(8,128)(2,1)}, u32[]{:S(2)}) %copy-start) | copy-done | bytes 2097176
  1.6 0.0 copy-start.1
  1.6 0.9 %copy-done.1 = bf16[512,128]{1,0:T(8,128)(2,1)S(1)} copy-done((bf16[512,128]{1,0:T(8,128)(2,1)S(1)}, bf16[512,128]{1,0:T(8,128)(2,1)}, u32[]{:S(2)}) %copy-start.1) | copy-done | bytes 131096
  2.5 0.0 copy-start.2
  2.5 0.9 %copy-done.2 = bf16[512,128]{1,0:T(8,128)(2,1)S(1)} copy-done((bf16[512,128]{1,0:T(8,128)(2,1)S(1)}, bf16[512,128]{1,0:T(8,128)(2,1)}, u32[]{:S(2)}) %copy-start.2) | copy-done | bytes 131096
  3.4 0.0 copy-start.3
  3.4 0.9 %copy-done.3 = bf16[512,128]{1,0:T(8,128)(2,1)S(1)} copy-done((bf16[512,128]{1,0:T(8,128)(2,1)S(1)}, bf16[512,128]{1,0:T(8,128)(2,1)}, u32[]{:S(2)}) %copy-start.3) | copy-done | bytes 131096
  4.3 0.0 copy-start.4
  4.3 0.9 %copy-done.4 = bf16[512,128]{1,0:T(8,128)(2,1)S(1)} copy-done((bf16[512,128]{1,0:T(8,128)(2,1)S(1)}, bf16[512,128]{1,0:T(8,128)(2,1)}, u32[]{:S(2)}) %copy-start.4) | copy-done | bytes 131096
  5.2 0.0 copy-start.5
  5.2 0.7 %copy-done.5 = f32[2,512]{1,0:T(2,128)S(1)} copy-done((f32[2,512]{1,0:T(2,128)S(1)}, f32[2,512]{1,0:T(2,128)}, u32[]{:S(2)}) %copy-start.5) | copy-done | bytes 4120
  5.9 53.2 %ssd_layer.1 = bf16[512,128]{1,0:T(8,128)(2,1)S(1)} custom-call(bf16[512,128]{1,0:T(8,128)(2,1)S(1)} %copy-done.1, bf16[512,128]{1,0:T(8,128)(2,1)S(1)} %copy-done.2, bf16[512,128]{1,0:T(8,128)(2,1)S(1)} %copy-done.3, bf16[512,128]{1,0:T(8,128)(2,1)S(1)} %copy-done.4, f32[2,512]{1,0:T(2,128)S(1)} %copy-done.5, bf16[8192,128]{1,0:T(8,128)(2,1)S(1)} %copy-done), custom_call_target="tpu_custom_call" | custom-call | tf_op jit(solution)/shard_map/ssd_layer/pallas_call | solution.py:274
  59.1 0.7 %copy.8 = bf16[512,128]{1,0:T(8,128)(2,1)} copy(bf16[512,128]{1,0:T(8,128)(2,1)S(1)} %ssd_layer.1) | data formatting | bytes 262144
Async XLA Ops:
  0.0 1.6 %copy-start = (bf16[8192,128]{1,0:T(8,128)(2,1)S(1)}, bf16[8192,128]{1,0:T(8,128)(2,1)}, u32[]{:S(2)}) copy-start(bf16[8192,128]{1,0:T(8,128)(2,1)} %w_ref.1) | copy-start | bytes 6291460
  1.6 0.9 %copy-start.1 = (bf16[512,128]{1,0:T(8,128)(2,1)S(1)}, bf16[512,128]{1,0:T(8,128)(2,1)}, u32[]{:S(2)}) copy-start(bf16[512,128]{1,0:T(8,128)(2,1)} %x_ref.1) | copy-start | bytes 393220
  2.5 0.9 %copy-start.2 = (bf16[512,128]{1,0:T(8,128)(2,1)S(1)}, bf16[512,128]{1,0:T(8,128)(2,1)}, u32[]{:S(2)}) copy-start(bf16[512,128]{1,0:T(8,128)(2,1)} %gate_ref.1) | copy-start | bytes 393220
  3.4 0.9 %copy-start.3 = (bf16[512,128]{1,0:T(8,128)(2,1)S(1)}, bf16[512,128]{1,0:T(8,128)(2,1)}, u32[]{:S(2)}) copy-start(bf16[512,128]{1,0:T(8,128)(2,1)} %b_ref.1) | copy-start | bytes 393220
  4.3 0.9 %copy-start.4 = (bf16[512,128]{1,0:T(8,128)(2,1)S(1)}, bf16[512,128]{1,0:T(8,128)(2,1)}, u32[]{:S(2)}) copy-start(bf16[512,128]{1,0:T(8,128)(2,1)} %c_ref.1) | copy-start | bytes 393220
  5.2 0.7 %copy-start.5 = (f32[2,512]{1,0:T(2,128)S(1)}, f32[2,512]{1,0:T(2,128)}, u32[]{:S(2)}) copy-start(f32[2,512]{1,0:T(2,128)} %decay_ref.1) | copy-start | bytes 12292

commit v2 on v1

--- a/solution.py
+++ b/solution.py
@@ -38,16 +38,22 @@
 
 def kernel(
     seq_size,
+    x_hbm,
+    gate_hbm,
+    b_hbm,
+    c_hbm,
+    decay_hbm,
+    w_ref,
+    out_ref,
     x_ref,
     gate_ref,
     b_ref,
     c_ref,
     decay_ref,
-    w_ref,
-    out_ref,
     m1,
     m2,
     m2_in,
+    start_ref,
     diag,
     wide,
     blocks,
@@ -59,9 +65,11 @@
     m1_r,
     m2_s,
     m2_r,
+    ready,
     w_s,
     w_r,
     own_s,
+    in_s,
     ring_s,
     ring_r,
     twin_s,
@@ -77,6 +85,7 @@
     head = lax.axis_index("head")
     px, py, core = head // (NY * NC), (head // NC) % NY, head % NC
     group, place = s // SPAN, s % SPAN
+    groups = seq_size // SPAN
 
     def device(z, x, y, c):
         return (z, (x * NY + y) * NC + c)
@@ -84,6 +93,7 @@
     mates = [(place + i) % SPAN for i in range(1, SPAN)]
     mate_ids = [device(group * SPAN + m, px, py, core) for m in mates]
     ahead_ids = [device((s + SPAN * i) % seq_size, px, py, core) for i in (1, 2)]
+    behind_ids = [device((s + seq_size - SPAN * i) % seq_size, px, py, core) for i in (1, 2)]
     peers = [(px + i) % NX for i in range(1, NX)]
     peer_ids = [device(s, p, py, core) for p in peers]
     up = device(s, px, (py + 1) % NY, core)
@@ -95,10 +105,34 @@
             src_ref=src, dst_ref=dst, send_sem=send, recv_sem=recv, device_id=to, device_id_type=MESH
         )
 
-    partners = mate_ids + ahead_ids + peer_ids + [up, down, twin]
+    loads = [
+        pltpu.make_async_copy(src, dst, in_s.at[i])
+        for i, (src, dst) in enumerate(
+            (
+                (decay_hbm, decay_ref),
+                (b_hbm, b_ref),
+                (x_hbm, x_ref),
+                (c_hbm, c_ref),
+                (gate_hbm, gate_ref),
+            )
+        )
+    ]
+    for load in loads:
+        load.start()
+
+    partners = mate_ids + peer_ids + [up, down, twin]
     barrier = pltpu.get_barrier_semaphore()
+
+    def signal(sem, to):
+        pl.semaphore_signal(sem, inc=1, device_id=to, device_id_type=MESH)
+
     for to in partners:
-        pl.semaphore_signal(barrier, inc=1, device_id=to, device_id_type=MESH)
+        signal(barrier, to)
+    for i, to in enumerate(ahead_ids):
+
+        @pl.when(group + i + 1 < groups)
+        def _():
+            signal(barrier, to)
 
     depth = NY * NC * columns
     own_w = pltpu.make_async_copy(w_ref.at[pl.ds(px * depth, depth), :], w_buf.at[px], own_s)
@@ -110,6 +144,8 @@
     first_head = lax.broadcasted_iota(jnp.int32, (BLOCK, columns), 1) < channels
     first_row = lax.broadcasted_iota(jnp.int32, (columns, BLOCK), 0) < channels
     local, cum_last = [], []
+    for load in loads[:3]:
+        load.wait()
     for q in range(rows // BLOCK):
         at = slice(q * BLOCK, (q + 1) * BLOCK)
         decay = decay_ref[:, at]
@@ -137,12 +173,21 @@
         jnp.exp(cum_last[0] + cum_last[1]),
     )
 
-    pl.semaphore_wait(barrier, len(partners))
+    pl.semaphore_wait(barrier, len(partners) + group)
     sent = []
     for i, to in enumerate(mate_ids):
         copy = remote(m1_own, m1_own, m1_s.at[i], m1_r.at[i], to)
-        copy.start()
-        sent.append(copy)
+
+        @pl.when((group < groups - 1) | (place + i + 1 < SPAN))
+        def _():
+            copy.start()
+
+    for i, to in enumerate(behind_ids):
+
+        @pl.when(group >= i + 1)
+        def _():
+            signal(ready.at[i], to)
+
     for i, to in enumerate(peer_ids):
         copy = remote(
             w_ref.at[pl.ds(peers[i] * depth, depth), :], w_buf.at[px], w_s.at[i], w_r.at[i], to
@@ -150,6 +195,8 @@
         copy.start()
         sent.append(copy)
 
+    for load in loads[3:]:
+        load.wait()
     for q in range(rows // BLOCK):
         at = slice(q * BLOCK, (q + 1) * BLOCK)
         decay = decay_ref[:, at]
@@ -166,7 +213,11 @@
 
     for i in range(SPAN - 1):
         slot = m1.at[(place + SPAN - 1 - i) % SPAN]
-        remote(slot, slot, m1_s.at[i], m1_r.at[i], mate_ids[i]).wait_recv()
+
+        @pl.when((group < groups - 1) | (place >= i + 1))
+        def _():
+            remote(slot, slot, m1_s.at[i], m1_r.at[i], mate_ids[i]).wait_recv()
+
     state = jnp.zeros((states, columns), F32)
     decayed = jnp.ones((1, columns), F32)
     before, before_decay = state, decayed
@@ -176,17 +227,35 @@
         more, its_decay = unpack(m1.at[i], states)
         state = state * its_decay + more
         decayed = decayed * its_decay
-    pack(m2, state, decayed)
+
+    @pl.when(group < groups - 1)
+    def _():
+        pack(m2, state, decayed)
+
     for i, to in enumerate(ahead_ids):
-        copy = remote(m2, m2_in.at[i], m2_s.at[i], m2_r.at[i], to)
-        copy.start()
-        sent.append(copy)
-    for i, to in enumerate(ahead_ids):
-        remote(m2, m2_in.at[i], m2_s.at[i], m2_r.at[i], to).wait_recv()
-    near, near_decay = unpack(m2_in.at[0], states)
-    far, _ = unpack(m2_in.at[1], states)
-    earlier = jnp.where(group >= 2, far * near_decay, 0.0) + near
-    start = before + jnp.where(group >= 1, earlier * before_decay, 0.0)
+
+        @pl.when(group + i + 1 < groups)
+        def _():
+            pl.semaphore_wait(ready.at[i], 1)
+            remote(m2, m2_in.at[i], m2_s.at[i], m2_r.at[i], to).start()
+
+    start_ref[...] = before
+
+    @pl.when(group == 1)
+    def _():
+        remote(m2, m2_in.at[0], m2_s.at[0], m2_r.at[0], ahead_ids[0]).wait_recv()
+        near, _ = unpack(m2_in.at[0], states)
+        start_ref[...] = before + near * before_decay
+
+    @pl.when(group == 2)
+    def _():
+        for i, to in enumerate(ahead_ids):
+            remote(m2, m2_in.at[i], m2_s.at[i], m2_r.at[i], to).wait_recv()
+        near, near_decay = unpack(m2_in.at[0], states)
+        far, _ = unpack(m2_in.at[1], states)
+        start_ref[...] = before + (far * near_decay + near) * before_decay
+
+    start = start_ref[...]
     starts = [start, start * jnp.exp(cum_last[0]) + local[0]]
 
     mine = py * NC + core
@@ -263,6 +332,17 @@
         out_ref[at, :] = value.astype(BF16)
     for copy in sent:
         copy.wait_send()
+    for i, to in enumerate(mate_ids):
+
+        @pl.when((group < groups - 1) | (place + i + 1 < SPAN))
+        def _():
+            remote(m1_own, m1_own, m1_s.at[i], m1_r.at[i], to).wait_send()
+
+    for i, to in enumerate(ahead_ids):
+
+        @pl.when(group + i + 1 < groups)
+        def _():
+            remote(m2, m2_in.at[i], m2_s.at[i], m2_r.at[i], to).wait_send()
 
 
 def per_device(seq_size, x_in, gate_in, b_in, c_in, log_decay, w_out):
@@ -273,13 +353,19 @@
     vmem = pl.BlockSpec(memory_space=pltpu.VMEM)
     return pl.pallas_call(
         functools.partial(kernel, seq_size),
-        out_shape=jax.ShapeDtypeStruct((rows, columns), BF16),
-        in_specs=[vmem] * 5 + [pl.BlockSpec(memory_space=pl.ANY)],
+        out_shape=pltpu.VMEM((rows, columns), BF16),
+        in_specs=[pl.BlockSpec(memory_space=pltpu.HBM)] * 6,
         out_specs=vmem,
         scratch_shapes=[
+            pltpu.VMEM((rows, columns), BF16),
+            pltpu.VMEM((rows, columns), BF16),
+            pltpu.VMEM((rows, states), BF16),
+            pltpu.VMEM((rows, states), BF16),
+            pltpu.VMEM(log_decay.shape, F32),
             pltpu.VMEM((SPAN, states + 16, columns), BF16),
             pltpu.VMEM((states + 16, columns), BF16),
             pltpu.VMEM((2, states + 16, columns), BF16),
+            pltpu.VMEM((states, columns), F32),
             pltpu.VMEM((rows, columns), F32),
             pltpu.VMEM((rows, columns), F32),
             pltpu.VMEM((NY * NC, rows, columns), BF16),
@@ -291,9 +377,11 @@
             dma((SPAN - 1,)),
             dma((2,)),
             dma((2,)),
+            pltpu.SemaphoreType.REGULAR((2,)),
             dma((NX - 1,)),
             dma((NX - 1,)),
             dma(()),
+            dma((5,)),
             dma((CHUNKS, 2, NY // 2)),
             dma((CHUNKS, 2, NY // 2)),
             dma((CHUNKS, NY)),
@@ -302,7 +390,7 @@
             dma((NX - 1, CHUNKS)),
         ],
         compiler_params=pltpu.CompilerParams(
-            collective_id=0, has_side_effects=True, vmem_limit_bytes=40 * 2**20
+            collective_id=0, has_side_effects=True, vmem_limit_bytes=56 * 2**20
         ),
         name="ssd_layer",
     )(x_in, gate_in, b_in, c_in, log_decay, w_out)

time: 60 us -> 46.5 us (0.78)
  Pallas kernels: 53.2 us -> 45.7 us
  local copies, waits for them, and re-layouts: 6.55 us -> 0.66 us
    pallas_call x1, Pallas kernels: 53.2 us -> 45.7 us  [per_device(): pl.pallas_call(functools.partial(kernel, seq_size), out_shape=pltpu.VMEM(...]
    unnamed x13 -> x1, local copies, waits for them, and re-layouts: 6.55 us -> 0.66 us
where the time goes in v2:
time: 46.5 us; the launch traced here: 46.3 us
  Pallas kernels  45.7 us (98%)
  local copies, waits for them, and re-layouts  0.66 us (1%)
    pallas_call x1, Pallas kernels, per_device(): pl.pallas_call(functools.partial(kernel, seq_size), out_shape=pltpu.VMEM(...  45.7 us

profile of v2, /device:TPU:1, one launch (start us, length us, event | category | flops | bytes accessed | tf_op | source)
XLA Modules:
  0.0 46.3 jit_solution(7007760547727507826)
XLA Ops:
  0.0 45.7 %ssd_layer.1 = bf16[512,128]{1,0:T(8,128)(2,1)S(1)} custom-call(bf16[512,128]{1,0:T(8,128)(2,1)} %x_hbm.1, bf16[512,128]{1,0:T(8,128)(2,1)} %gate_hbm.1, bf16[512,128]{1,0:T(8,128)(2,1)} %b_hbm.1, bf16[512,128]{1,0:T(8,128)(2,1)} %c_hbm.1, f32[2,512]{1,0:T(2,128)} %decay_hbm.1, bf16[8192,128]{1,0:T(8,128)(2,1)} %w_ref.1), custom_call_target="tpu_custom_call" | custom-call | tf_op jit(solution)/shard_map/ssd_layer/pallas_call | solution.py:354
  45.7 0.7 %copy.8 = bf16[512,128]{1,0:T(8,128)(2,1)} copy(bf16[512,128]{1,0:T(8,128)(2,1)S(1)} %ssd_layer.1) | data formatting | bytes 262144

commit v3 on v2

--- a/solution.py
+++ b/solution.py
@@ -50,9 +50,9 @@
     b_ref,
     c_ref,
     decay_ref,
-    m1,
+    own_state,
     m2,
-    m2_in,
+    state_in,
     start_ref,
     diag,
     wide,
@@ -68,6 +68,8 @@
     ready,
     w_s,
     w_r,
+    swap_s,
+    swap_r,
     own_s,
     in_s,
     ring_s,
@@ -84,16 +86,26 @@
     s = lax.axis_index("seq")
     head = lax.axis_index("head")
     px, py, core = head // (NY * NC), (head // NC) % NY, head % NC
-    group, place = s // SPAN, s % SPAN
+    group, place, odd = s // SPAN, s % SPAN, s % 2
     groups = seq_size // SPAN
+    opening = group == 0
 
     def device(z, x, y, c):
         return (z, (x * NY + y) * NC + c)
 
-    mates = [(place + i) % SPAN for i in range(1, SPAN)]
-    mate_ids = [device(group * SPAN + m, px, py, core) for m in mates]
-    ahead_ids = [device((s + SPAN * i) % seq_size, px, py, core) for i in (1, 2)]
-    behind_ids = [device((s + seq_size - SPAN * i) % seq_size, px, py, core) for i in (1, 2)]
+    mate = device(s + 1 - 2 * odd, px, py, core)
+    def after(i):
+        return device((s + i) % seq_size, px, py, core)
+
+    mates = [device(group * SPAN + (place + i) % SPAN, px, py, core) for i in range(1, SPAN)]
+    to_mates = [opening | (odd == 0) if i == 0 else opening for i in range(SPAN - 1)]
+    from_mates = [opening | (odd == 1) if i == 0 else opening for i in range(SPAN - 1)]
+    pair_end = (group > 0) & (place == 1)
+    group_end = (group == 1) & (place == SPAN - 1)
+    late_pair, late, closing = (group > 0) & (place >= 2), group > 0, group == groups - 1
+    pair_from = device(group * SPAN + 1, px, py, core)
+    group_from = device(2 * SPAN - 1, px, py, core)
+    opening_from = device(place, px, py, core)
     peers = [(px + i) % NX for i in range(1, NX)]
     peer_ids = [device(s, p, py, core) for p in peers]
     up = device(s, px, (py + 1) % NY, core)
@@ -120,7 +132,7 @@
     for load in loads:
         load.start()
 
-    partners = mate_ids + peer_ids + [up, down, twin]
+    partners = peer_ids + [up, down, twin]
     barrier = pltpu.get_barrier_semaphore()
 
     def signal(sem, to):
@@ -128,13 +140,64 @@
 
     for to in partners:
         signal(barrier, to)
-    for i, to in enumerate(ahead_ids):
-
-        @pl.when(group + i + 1 < groups)
+    sends = [(opening, after(SPAN * i), i - 1, 2) for i in (1, 2)]
+    sends += [(pair_end, after(i), i - 1, 0) for i in (1, 2)]
+    sends += [(group_end, after(i), i - 1, 1) for i in (1, 2, 3, 4)]
+    for use, to, _, _ in sends:
+
+        @pl.when(use)
         def _():
             signal(barrier, to)
 
+    @pl.when(opening)
+    def _():
+        for i in range(1, SPAN):
+            signal(barrier, mates[i - 1])
+
+    @pl.when(late)
+    def _():
+        signal(barrier, mate)
+
+    greetings = jnp.where(opening, SPAN - 1, 2 + place // 2 + group // 2)
+    pl.semaphore_wait(barrier, len(partners) + greetings)
+
+    @pl.when(late)
+    def _():
+        signal(ready.at[group - 1], opening_from)
+
+    @pl.when(late_pair)
+    def _():
+        signal(ready.at[place - 2], pair_from)
+
+    @pl.when(closing)
+    def _():
+        signal(ready.at[place], group_from)
+
+    sent = []
     depth = NY * NC * columns
+    half = depth // 2
+    for i in (1, 0, 2):
+        at, n = (odd * half, half) if i == 1 else (0, depth)
+        copy = remote(
+            w_ref.at[pl.ds(peers[i] * depth + at, n), :],
+            w_buf.at[px, pl.ds(at, n)],
+            w_s.at[i],
+            w_r.at[i],
+            peer_ids[i],
+        )
+        copy.start()
+        sent.append(copy)
+    opposite = (px + NX // 2) % NX
+
+    def swap(mine):
+        slot = w_buf.at[opposite, pl.ds((odd if mine else 1 - odd) * half, half)]
+        return slot, remote(slot, slot, swap_s, swap_r, mate)
+
+    def start_swap():
+        slot, copy = swap(True)
+        remote(slot, slot, w_s.at[1], w_r.at[1], peer_ids[1]).wait_recv()
+        copy.start()
+
     own_w = pltpu.make_async_copy(w_ref.at[pl.ds(px * depth, depth), :], w_buf.at[px], own_s)
     own_w.start()
     t_of = lax.broadcasted_iota(jnp.int32, (BLOCK, BLOCK), 0)
@@ -166,34 +229,21 @@
         ]
         local.append(jnp.where(first_head[:states], halves[0], halves[1]))
         cum_last.append(last)
-    m1_own = m1.at[place]
     pack(
-        m1_own,
+        own_state.at[place],
         local[0] * jnp.exp(cum_last[1]) + local[1],
         jnp.exp(cum_last[0] + cum_last[1]),
     )
 
-    pl.semaphore_wait(barrier, len(partners) + group)
-    sent = []
-    for i, to in enumerate(mate_ids):
-        copy = remote(m1_own, m1_own, m1_s.at[i], m1_r.at[i], to)
-
-        @pl.when((group < groups - 1) | (place + i + 1 < SPAN))
+    def to_mate(i):
+        slot = own_state.at[place]
+        return remote(slot, slot, m1_s.at[i], m1_r.at[i], mates[i])
+
+    for i in range(SPAN - 1):
+
+        @pl.when(to_mates[i])
         def _():
-            copy.start()
-
-    for i, to in enumerate(behind_ids):
-
-        @pl.when(group >= i + 1)
-        def _():
-            signal(ready.at[i], to)
-
-    for i, to in enumerate(peer_ids):
-        copy = remote(
-            w_ref.at[pl.ds(peers[i] * depth, depth), :], w_buf.at[px], w_s.at[i], w_r.at[i], to
-        )
-        copy.start()
-        sent.append(copy)
+            to_mate(i).start()
 
     for load in loads[3:]:
         load.wait()
@@ -211,49 +261,81 @@
             halves.append(jnp.dot(weights.astype(BF16), x, preferred_element_type=F32))
         diag[at, :] = jnp.where(first_head, halves[0], halves[1])
 
+    def send(chosen):
+        for use, to, i, k in chosen:
+
+            @pl.when(use)
+            def _():
+                pl.semaphore_wait(ready.at[i], 1)
+                remote(m2, state_in.at[k], m2_s.at[i], m2_r.at[k], to).start()
+
+    def state_from(k):
+        remote(m2, state_in.at[k], m2_s.at[0], m2_r.at[k], mate).wait_recv()
+        return unpack(state_in.at[k], states)
+
     for i in range(SPAN - 1):
-        slot = m1.at[(place + SPAN - 1 - i) % SPAN]
-
-        @pl.when((group < groups - 1) | (place >= i + 1))
+
+        @pl.when(from_mates[i])
         def _():
-            remote(slot, slot, m1_s.at[i], m1_r.at[i], mate_ids[i]).wait_recv()
-
-    state = jnp.zeros((states, columns), F32)
-    decayed = jnp.ones((1, columns), F32)
-    before, before_decay = state, decayed
-    for i in range(SPAN):
-        before = jnp.where(place == i, state, before)
-        before_decay = jnp.where(place == i, decayed, before_decay)
-        more, its_decay = unpack(m1.at[i], states)
-        state = state * its_decay + more
-        decayed = decayed * its_decay
-
-    @pl.when(group < groups - 1)
-    def _():
-        pack(m2, state, decayed)
-
-    for i, to in enumerate(ahead_ids):
-
-        @pl.when(group + i + 1 < groups)
-        def _():
-            pl.semaphore_wait(ready.at[i], 1)
-            remote(m2, m2_in.at[i], m2_s.at[i], m2_r.at[i], to).start()
-
-    start_ref[...] = before
-
-    @pl.when(group == 1)
-    def _():
-        remote(m2, m2_in.at[0], m2_s.at[0], m2_r.at[0], ahead_ids[0]).wait_recv()
-        near, _ = unpack(m2_in.at[0], states)
-        start_ref[...] = before + near * before_decay
-
-    @pl.when(group == 2)
-    def _():
-        for i, to in enumerate(ahead_ids):
-            remote(m2, m2_in.at[i], m2_s.at[i], m2_r.at[i], to).wait_recv()
-        near, near_decay = unpack(m2_in.at[0], states)
-        far, _ = unpack(m2_in.at[1], states)
-        start_ref[...] = before + (far * near_decay + near) * before_decay
+            slot = own_state.at[(place + SPAN - 1 - i) % SPAN]
+            remote(slot, slot, m1_s.at[i], m1_r.at[i], mates[i]).wait_recv()
+
+    @pl.when(opening)
+    def _():
+        state = jnp.zeros((states, columns), F32)
+        before = state
+        decay = jnp.ones((1, columns), F32)
+        for i in range(SPAN):
+            before = jnp.where(place == i, state, before)
+            more, its_decay = unpack(own_state.at[i], states)
+            state = state * its_decay + more
+            decay = decay * its_decay
+        pack(m2, state, decay)
+        start_ref[...] = before
+
+    send(sends[:1])
+
+    def joined():
+        state, decay = unpack(own_state.at[place], states)
+        more, its_decay = unpack(own_state.at[jnp.maximum(place - 1, 0)], states)
+        return more * decay + state, decay * its_decay
+
+    @pl.when(pair_end)
+    def _():
+        pack(m2, *joined())
+
+    send(sends[2:4])
+
+    @pl.when(group_end)
+    def _():
+        state, decay = joined()
+        more, its_decay = state_from(0)
+        pack(m2, more * decay + state, decay * its_decay)
+
+    send(sends[4:])
+
+    @pl.when(late)
+    def _():
+        start_ref[...] = state_from(2)[0]
+
+    @pl.when(closing)
+    def _():
+        more, its_decay = state_from(1)
+        start_ref[...] = start_ref[...] * its_decay + more
+
+    @pl.when(late_pair & jnp.logical_not(group_end))
+    def _():
+        state_from(0)
+
+    @pl.when(late_pair)
+    def _():
+        more, its_decay = unpack(state_in.at[0], states)
+        start_ref[...] = start_ref[...] * its_decay + more
+
+    @pl.when(late & (odd == 1))
+    def _():
+        more, its_decay = unpack(own_state.at[jnp.maximum(place - 1, 0)], states)
+        start_ref[...] = start_ref[...] * its_decay + more
 
     start = start_ref[...]
     starts = [start, start * jnp.exp(cum_last[0]) + local[0]]
@@ -275,6 +357,12 @@
         copy.start()
         sent.append(copy)
 
+    send(sends[1:2])
+
+    @pl.when(group > 0)
+    def _():
+        start_swap()
+
     def hops(r, d):
         return NY // 2 if (r + d) % 2 == 0 else NY // 2 - 1
 
@@ -282,6 +370,12 @@
         return (py + NY - hop) % NY if d == 0 else (py + hop) % NY
 
     for hop in range(1, NY // 2 + 1):
+        if hop == 2:
+
+            @pl.when(group == 0)
+            def _():
+                start_swap()
+
         for r in range(CHUNKS):
             at = slice(r * step, (r + 1) * step)
             for d, to in enumerate((up, down)):
@@ -299,9 +393,10 @@
                 sent.append(copy)
 
     own_w.wait()
-    for i in range(NX - 1):
+    for i in (0, 2):
         slot = w_buf.at[(px + NX - 1 - i) % NX]
         remote(slot, slot, w_s.at[i], w_r.at[i], peer_ids[i]).wait_recv()
+    swap(False)[1].wait_recv()
     for r in range(CHUNKS):
         at = slice(r * step, (r + 1) * step)
         for which in range(NY):
@@ -332,17 +427,19 @@
         out_ref[at, :] = value.astype(BF16)
     for copy in sent:
         copy.wait_send()
-    for i, to in enumerate(mate_ids):
-
-        @pl.when((group < groups - 1) | (place + i + 1 < SPAN))
+
+    for i in range(SPAN - 1):
+
+        @pl.when(to_mates[i])
         def _():
-            remote(m1_own, m1_own, m1_s.at[i], m1_r.at[i], to).wait_send()
-
-    for i, to in enumerate(ahead_ids):
-
-        @pl.when(group + i + 1 < groups)
+            to_mate(i).wait_send()
+
+    swap(True)[1].wait_send()
+    for use, to, i, k in sends:
+
+        @pl.when(use)
         def _():
-            remote(m2, m2_in.at[i], m2_s.at[i], m2_r.at[i], to).wait_send()
+            remote(m2, state_in.at[k], m2_s.at[i], m2_r.at[k], to).wait_send()
 
 
 def per_device(seq_size, x_in, gate_in, b_in, c_in, log_decay, w_out):
@@ -364,7 +461,7 @@
             pltpu.VMEM(log_decay.shape, F32),
             pltpu.VMEM((SPAN, states + 16, columns), BF16),
             pltpu.VMEM((states + 16, columns), BF16),
-            pltpu.VMEM((2, states + 16, columns), BF16),
+            pltpu.VMEM((3, states + 16, columns), BF16),
             pltpu.VMEM((states, columns), F32),
             pltpu.VMEM((rows, columns), F32),
             pltpu.VMEM((rows, columns), F32),
@@ -375,11 +472,13 @@
             pltpu.VMEM((NX - 1, rows, columns), BF16),
             dma((SPAN - 1,)),
             dma((SPAN - 1,)),
-            dma((2,)),
-            dma((2,)),
-            pltpu.SemaphoreType.REGULAR((2,)),
+            dma((SPAN,)),
+            dma((3,)),
+            pltpu.SemaphoreType.REGULAR((SPAN,)),
             dma((NX - 1,)),
             dma((NX - 1,)),
+            dma(()),
+            dma(()),
             dma(()),
             dma((5,)),
             dma((CHUNKS, 2, NY // 2)),

time: 46.5 us -> 42.8 us (0.920)
  the two profiles are of different devices: /device:TPU:1 before, /device:TPU:704 now
where the time goes in v3:
time: 42.8 us; the launch traced here: 42.6 us
  Pallas kernels  42 us (98%)
  local copies, waits for them, and re-layouts  0.66 us (2%)
    pallas_call x1, Pallas kernels, per_device(): pl.pallas_call(functools.partial(kernel, seq_size), out_shape=pltpu.VMEM(...  42 us

profile of v3, /device:TPU:704, one launch (start us, length us, event | category | flops | bytes accessed | tf_op | source)
XLA Modules:
  0.0 42.6 jit_solution(18383875821523499336)
XLA Ops:
  0.0 42.0 %ssd_layer.1 = bf16[512,128]{1,0:T(8,128)(2,1)S(1)} custom-call(bf16[512,128]{1,0:T(8,128)(2,1)} %x_hbm.1, bf16[512,128]{1,0:T(8,128)(2,1)} %gate_hbm.1, bf16[512,128]{1,0:T(8,128)(2,1)} %b_hbm.1, bf16[512,128]{1,0:T(8,128)(2,1)} %c_hbm.1, f32[2,512]{1,0:T(2,128)} %decay_hbm.1, bf16[8192,128]{1,0:T(8,128)(2,1)} %w_ref.1), custom_call_target="tpu_custom_call" | custom-call | tf_op jit(solution)/shard_map/ssd_layer/pallas_call | solution.py:451
  42.0 0.7 %copy.8 = bf16[512,128]{1,0:T(8,128)(2,1)} copy(bf16[512,128]{1,0:T(8,128)(2,1)S(1)} %ssd_layer.1) | data formatting | bytes 262144

commit v4 on v3

--- a/solution.py
+++ b/solution.py
@@ -99,7 +99,9 @@
 
     mates = [device(group * SPAN + (place + i) % SPAN, px, py, core) for i in range(1, SPAN)]
     to_mates = [opening | (odd == 0) if i == 0 else opening for i in range(SPAN - 1)]
-    from_mates = [opening | (odd == 1) if i == 0 else opening for i in range(SPAN - 1)]
+    from_mates = [
+        (opening & (place >= i + 1)) | ((odd == 1) if i == 0 else False) for i in range(SPAN - 1)
+    ]
     pair_end = (group > 0) & (place == 1)
     group_end = (group == 1) & (place == SPAN - 1)
     late_pair, late, closing = (group > 0) & (place >= 2), group > 0, group == groups - 1
@@ -159,34 +161,9 @@
         signal(barrier, mate)
 
     greetings = jnp.where(opening, SPAN - 1, 2 + place // 2 + group // 2)
-    pl.semaphore_wait(barrier, len(partners) + greetings)
-
-    @pl.when(late)
-    def _():
-        signal(ready.at[group - 1], opening_from)
-
-    @pl.when(late_pair)
-    def _():
-        signal(ready.at[place - 2], pair_from)
-
-    @pl.when(closing)
-    def _():
-        signal(ready.at[place], group_from)
-
     sent = []
     depth = NY * NC * columns
     half = depth // 2
-    for i in (1, 0, 2):
-        at, n = (odd * half, half) if i == 1 else (0, depth)
-        copy = remote(
-            w_ref.at[pl.ds(peers[i] * depth + at, n), :],
-            w_buf.at[px, pl.ds(at, n)],
-            w_s.at[i],
-            w_r.at[i],
-            peer_ids[i],
-        )
-        copy.start()
-        sent.append(copy)
     opposite = (px + NX // 2) % NX
 
     def swap(mine):
@@ -210,6 +187,32 @@
     for load in loads[:3]:
         load.wait()
     for q in range(rows // BLOCK):
+        if q == 1:
+            pl.semaphore_wait(barrier, len(partners) + greetings)
+
+            @pl.when(late)
+            def _():
+                signal(ready.at[group - 1], opening_from)
+
+            @pl.when(late_pair)
+            def _():
+                signal(ready.at[place - 2], pair_from)
+
+            @pl.when(closing)
+            def _():
+                signal(ready.at[place], group_from)
+
+            for i in (1, 0, 2):
+                at, n = (odd * half, half) if i == 1 else (0, depth)
+                copy = remote(
+                    w_ref.at[pl.ds(peers[i] * depth + at, n), :],
+                    w_buf.at[px, pl.ds(at, n)],
+                    w_s.at[i],
+                    w_r.at[i],
+                    peer_ids[i],
+                )
+                copy.start()
+                sent.append(copy)
         at = slice(q * BLOCK, (q + 1) * BLOCK)
         decay = decay_ref[:, at]
         cum = exact(ones, jnp.where(first_row, decay[0:1], decay[1:2]))
@@ -259,7 +262,10 @@
             gap = cum[:, h * channels : h * channels + 1] - along[8 * h : 8 * h + 1, :]
             weights = jnp.where(lower, scores * jnp.exp(jnp.where(lower, gap, 0.0)), 0.0)
             halves.append(jnp.dot(weights.astype(BF16), x, preferred_element_type=F32))
-        diag[at, :] = jnp.where(first_head, halves[0], halves[1])
+        gate = gate_ref[at, :].astype(F32)
+        gate = gate / (1.0 + jnp.exp(-gate))
+        diag[at, :] = jnp.where(first_head, halves[0], halves[1]) * gate
+        wide[at, :] = jnp.exp(cum) * gate
 
     def send(chosen):
         for use, to, i, k in chosen:
@@ -273,27 +279,39 @@
         remote(m2, state_in.at[k], m2_s.at[0], m2_r.at[k], mate).wait_recv()
         return unpack(state_in.at[k], states)
 
+    def wait_mates(chosen):
+        for i in range(SPAN - 1):
+
+            @pl.when(chosen[i])
+            def _():
+                slot = own_state.at[(place + SPAN - 1 - i) % SPAN]
+                remote(slot, slot, m1_s.at[i], m1_r.at[i], mates[i]).wait_recv()
+
+    wait_mates(from_mates)
+
+    @pl.when(opening)
+    def _():
+        start_ref[...] = jnp.zeros_like(start_ref)
+
     for i in range(SPAN - 1):
 
-        @pl.when(from_mates[i])
+        @pl.when(opening & (place > i))
         def _():
-            slot = own_state.at[(place + SPAN - 1 - i) % SPAN]
-            remote(slot, slot, m1_s.at[i], m1_r.at[i], mates[i]).wait_recv()
-
-    @pl.when(opening)
-    def _():
-        state = jnp.zeros((states, columns), F32)
-        before = state
-        decay = jnp.ones((1, columns), F32)
-        for i in range(SPAN):
-            before = jnp.where(place == i, state, before)
             more, its_decay = unpack(own_state.at[i], states)
-            state = state * its_decay + more
-            decay = decay * its_decay
-        pack(m2, state, decay)
-        start_ref[...] = before
-
-    send(sends[:1])
+            start_ref[...] = start_ref[...] * its_decay + more
+
+    def send_total(use):
+        @pl.when(use)
+        def _():
+            state, decay = unpack(own_state.at[0], states)
+            for i in range(1, SPAN):
+                more, its_decay = unpack(own_state.at[i], states)
+                state, decay = state * its_decay + more, decay * its_decay
+            pack(m2, state, decay)
+
+        send([(use, to, i, k) for _, to, i, k in sends[:1]])
+
+    send_total(opening & (place == SPAN - 1))
 
     def joined():
         state, decay = unpack(own_state.at[place], states)
@@ -345,9 +363,7 @@
         at = slice(r * step, (r + 1) * step)
         start_bf = starts[r * step // BLOCK].astype(BF16)
         carry = jnp.dot(c_ref[at, :], start_bf, preferred_element_type=F32)
-        y = diag[at, :] + carry * jnp.exp(wide[at, :])
-        gate = gate_ref[at, :].astype(F32)
-        blocks[mine, at, :] = (y * (gate / (1.0 + jnp.exp(-gate)))).astype(BF16)
+        blocks[mine, at, :] = (diag[at, :] + carry * wide[at, :]).astype(BF16)
         here = blocks.at[mine, at]
         for d, to in enumerate((up, down)):
             copy = remote(here, here, ring_s.at[r, d, 0], ring_r.at[r, d, 0], to)
@@ -357,11 +373,9 @@
         copy.start()
         sent.append(copy)
 
+    wait_mates([opening & (place < i + 1) for i in range(SPAN - 1)])
+    send_total(opening & (place < SPAN - 1))
     send(sends[1:2])
-
-    @pl.when(group > 0)
-    def _():
-        start_swap()
 
     def hops(r, d):
         return NY // 2 if (r + d) % 2 == 0 else NY // 2 - 1
@@ -372,9 +386,7 @@
     for hop in range(1, NY // 2 + 1):
         if hop == 2:
 
-            @pl.when(group == 0)
-            def _():
-                start_swap()
+            start_swap()
 
         for r in range(CHUNKS):
             at = slice(r * step, (r + 1) * step)
@@ -409,14 +421,20 @@
             there = blocks.at[where * NC + 1 - core, at]
             remote(there, there, twin_s.at[r, which], twin_r.at[r, which], twin).wait_recv()
         gathered = jnp.concatenate([blocks[k, at, :] for k in range(NY * NC)], axis=1)
-        for i, to in enumerate(peer_ids):
-            part[i, at, :] = jnp.dot(
-                gathered, w_buf[peers[i]], preferred_element_type=F32
-            ).astype(BF16)
-            copy = remote(part.at[i, at], part_in.at[i, at], part_s.at[i, r], part_r.at[i, r], to)
-            copy.start()
-            sent.append(copy)
-        total[at, :] = jnp.dot(gathered, w_buf[px], preferred_element_type=F32)
+        for pair in ((1, 0), (2, None)):
+            ws = [w_buf[px if i is None else peers[i]] for i in pair]
+            both = jnp.dot(gathered, jnp.concatenate(ws, axis=1), preferred_element_type=F32)
+            for k, i in enumerate(pair):
+                value = both[:, k * columns : (k + 1) * columns]
+                if i is None:
+                    total[at, :] = value
+                    continue
+                part[i, at, :] = value.astype(BF16)
+                copy = remote(
+                    part.at[i, at], part_in.at[i, at], part_s.at[i, r], part_r.at[i, r], peer_ids[i]
+                )
+                copy.start()
+                sent.append(copy)
     for r in range(CHUNKS):
         at = slice(r * step, (r + 1) * step)
         for i, to in enumerate(peer_ids):

time: 42.8 us -> 41.7 us (0.974)
  the two profiles are of different devices: /device:TPU:704 before, /device:TPU:1 now
where the time goes in v4:
time: 41.7 us; the launch traced here: 41.2 us
  Pallas kernels  40.6 us (97%)
  local copies, waits for them, and re-layouts  0.66 us (2%)
    pallas_call x1, Pallas kernels, per_device(): pl.pallas_call(functools.partial(kernel, seq_size), out_shape=pltpu.VMEM(...  40.6 us

profile of v4, /device:TPU:1, one launch (start us, length us, event | category | flops | bytes accessed | tf_op | source)
XLA Modules:
  0.0 41.2 jit_solution(1139264253541216068)
XLA Ops:
  0.0 40.6 %ssd_layer.1 = bf16[512,128]{1,0:T(8,128)(2,1)S(1)} custom-call(bf16[512,128]{1,0:T(8,128)(2,1)} %x_hbm.1, bf16[512,128]{1,0:T(8,128)(2,1)} %gate_hbm.1, bf16[512,128]{1,0:T(8,128)(2,1)} %b_hbm.1, bf16[512,128]{1,0:T(8,128)(2,1)} %c_hbm.1, f32[2,512]{1,0:T(2,128)} %decay_hbm.1, bf16[8192,128]{1,0:T(8,128)(2,1)} %w_ref.1), custom_call_target="tpu_custom_call" | custom-call | tf_op jit(solution)/shard_map/ssd_layer/pallas_call | solution.py:469
  40.6 0.7 %copy.8 = bf16[512,128]{1,0:T(8,128)(2,1)} copy(bf16[512,128]{1,0:T(8,128)(2,1)S(1)} %ssd_layer.1) | data formatting | bytes 262144

commit v5 on v4

--- a/solution.py
+++ b/solution.py
@@ -144,7 +144,7 @@
         signal(barrier, to)
     sends = [(opening, after(SPAN * i), i - 1, 2) for i in (1, 2)]
     sends += [(pair_end, after(i), i - 1, 0) for i in (1, 2)]
-    sends += [(group_end, after(i), i - 1, 1) for i in (1, 2, 3, 4)]
+    sends += [(group_end, after(i), i - 1, 1) for i in (2, 1, 4, 3)]
     for use, to, _, _ in sends:
 
         @pl.when(use)
@@ -383,33 +383,14 @@
     def behind(hop, d):
         return (py + NY - hop) % NY if d == 0 else (py + hop) % NY
 
-    for hop in range(1, NY // 2 + 1):
-        if hop == 2:
-
-            start_swap()
-
-        for r in range(CHUNKS):
-            at = slice(r * step, (r + 1) * step)
-            for d, to in enumerate((up, down)):
-                if hop > hops(r, d):
-                    continue
-                here = blocks.at[behind(hop, d) * NC + core, at]
-                remote(here, here, ring_s.at[r, d, hop - 1], ring_r.at[r, d, hop - 1], to).wait_recv()
-                if hop < hops(r, d):
-                    copy = remote(here, here, ring_s.at[r, d, hop], ring_r.at[r, d, hop], to)
-                    copy.start()
-                    sent.append(copy)
-                which = 2 * hop - 1 + d if hop < NY // 2 else NY - 1
-                copy = remote(here, here, twin_s.at[r, which], twin_r.at[r, which], twin)
-                copy.start()
-                sent.append(copy)
-
-    own_w.wait()
-    for i in (0, 2):
-        slot = w_buf.at[(px + NX - 1 - i) % NX]
-        remote(slot, slot, w_s.at[i], w_r.at[i], peer_ids[i]).wait_recv()
-    swap(False)[1].wait_recv()
-    for r in range(CHUNKS):
+    def wait_w():
+        own_w.wait()
+        for i in (0, 2):
+            slot = w_buf.at[(px + NX - 1 - i) % NX]
+            remote(slot, slot, w_s.at[i], w_r.at[i], peer_ids[i]).wait_recv()
+        swap(False)[1].wait_recv()
+
+    def product(r):
         at = slice(r * step, (r + 1) * step)
         for which in range(NY):
             if which == 0:
@@ -435,6 +416,35 @@
                 )
                 copy.start()
                 sent.append(copy)
+
+    for hop in range(1, NY // 2 + 1):
+        if hop == 2:
+
+            start_swap()
+
+        for r in range(CHUNKS):
+            at = slice(r * step, (r + 1) * step)
+            arrived = []
+            for d, to in enumerate((up, down)):
+                if hop > hops(r, d):
+                    continue
+                here = blocks.at[behind(hop, d) * NC + core, at]
+                remote(here, here, ring_s.at[r, d, hop - 1], ring_r.at[r, d, hop - 1], to).wait_recv()
+                if hop < hops(r, d):
+                    copy = remote(here, here, ring_s.at[r, d, hop], ring_r.at[r, d, hop], to)
+                    copy.start()
+                    sent.append(copy)
+                arrived.append((d, here))
+            for d, here in arrived:
+                which = 2 * hop - 1 + d if hop < NY // 2 else NY - 1
+                copy = remote(here, here, twin_s.at[r, which], twin_r.at[r, which], twin)
+                copy.start()
+                sent.append(copy)
+            if hop == NY // 2 and r == 1:
+                wait_w()
+            if hop == NY // 2 and r >= 1:
+                product(r - 1)
+    product(CHUNKS - 1)
     for r in range(CHUNKS):
         at = slice(r * step, (r + 1) * step)
         for i, to in enumerate(peer_ids):

time: 41.7 us -> 41.5 us (level)
  no operation moved by 1% of the time
where the time goes in v5:
time: 41.5 us; the launch traced here: 41.2 us
  Pallas kernels  40.6 us (98%)
  local copies, waits for them, and re-layouts  0.66 us (2%)
    pallas_call x1, Pallas kernels, per_device(): pl.pallas_call(functools.partial(kernel, seq_size), out_shape=pltpu.VMEM(...  40.6 us

profile of v5, /device:TPU:1, one launch (start us, length us, event | category | flops | bytes accessed | tf_op | source)
XLA Modules:
  0.0 41.2 jit_solution(15935235563266829405)
XLA Ops:
  0.0 40.6 %ssd_layer.1 = bf16[512,128]{1,0:T(8,128)(2,1)S(1)} custom-call(bf16[512,128]{1,0:T(8,128)(2,1)} %x_hbm.1, bf16[512,128]{1,0:T(8,128)(2,1)} %gate_hbm.1, bf16[512,128]{1,0:T(8,128)(2,1)} %b_hbm.1, bf16[512,128]{1,0:T(8,128)(2,1)} %c_hbm.1, f32[2,512]{1,0:T(2,128)} %decay_hbm.1, bf16[8192,128]{1,0:T(8,128)(2,1)} %w_ref.1), custom_call_target="tpu_custom_call" | custom-call | tf_op jit(solution)/shard_map/ssd_layer/pallas_call | solution.py:479
  40.6 0.7 %copy.8 = bf16[512,128]{1,0:T(8,128)(2,1)} copy(bf16[512,128]{1,0:T(8,128)(2,1)S(1)} %ssd_layer.1) | data formatting | bytes 262144

commit v6 on v5

--- a/solution.py
+++ b/solution.py
@@ -175,8 +175,6 @@
         remote(slot, slot, w_s.at[1], w_r.at[1], peer_ids[1]).wait_recv()
         copy.start()
 
-    own_w = pltpu.make_async_copy(w_ref.at[pl.ds(px * depth, depth), :], w_buf.at[px], own_s)
-    own_w.start()
     t_of = lax.broadcasted_iota(jnp.int32, (BLOCK, BLOCK), 0)
     s_of = lax.broadcasted_iota(jnp.int32, (BLOCK, BLOCK), 1)
     lower = s_of <= t_of
@@ -248,6 +246,8 @@
         def _():
             to_mate(i).start()
 
+    own_w = pltpu.make_async_copy(w_ref.at[pl.ds(px * depth, depth), :], w_buf.at[px], own_s)
+    own_w.start()
     for load in loads[3:]:
         load.wait()
     for q in range(rows // BLOCK):

time: 41.5 us -> 41.5 us (level)
  no operation moved by 1% of the time
where the time goes in v6:
time: 41.5 us; the launch traced here: 41.2 us
  Pallas kernels  40.6 us (98%)
  local copies, waits for them, and re-layouts  0.66 us (2%)
    pallas_call x1, Pallas kernels, per_device(): pl.pallas_call(functools.partial(kernel, seq_size), out_shape=pltpu.VMEM(...  40.6 us

profile of v6, /device:TPU:1, one launch (start us, length us, event | category | flops | bytes accessed | tf_op | source)
XLA Modules:
  0.0 41.2 jit_solution(15260057853687660603)
XLA Ops:
  0.0 40.6 %ssd_layer.1 = bf16[512,128]{1,0:T(8,128)(2,1)S(1)} custom-call(bf16[512,128]{1,0:T(8,128)(2,1)} %x_hbm.1, bf16[512,128]{1,0:T(8,128)(2,1)} %gate_hbm.1, bf16[512,128]{1,0:T(8,128)(2,1)} %b_hbm.1, bf16[512,128]{1,0:T(8,128)(2,1)} %c_hbm.1, f32[2,512]{1,0:T(2,128)} %decay_hbm.1, bf16[8192,128]{1,0:T(8,128)(2,1)} %w_ref.1), custom_call_target="tpu_custom_call" | custom-call | tf_op jit(solution)/shard_map/ssd_layer/pallas_call | solution.py:479
  40.6 0.7 %copy.8 = bf16[512,128]{1,0:T(8,128)(2,1)} copy(bf16[512,128]{1,0:T(8,128)(2,1)S(1)} %ssd_layer.1) | data formatting | bytes 262144
